TPU v7x, 512 devices: a whole 4x4x16 slice. The times are simulated.
512 devices in a mesh: row: 16 (over z), col: 32 (over x, y, core).
Axes of the slice: x: 4, y: 4, z: 16, core: 2. Of those that a mesh axis runs over, the one named last changes fastest.
Arguments:
- band: float32 [12288, 24576], P('col', 'row'), may hold values from -6 to 6
- band_pattern: int32 [96, 192], P('col', 'row'), may hold values 0 or 1
- slab: float32 [24576, 8192], P('col', 'row'), may hold values from -0.25 to 0.25
- slab_pattern: int32 [192, 64], P('col', 'row'), may hold values 0 or 1
Outputs:
- product: float32 [12288, 8192], P('col', 'row')
All inputs are finite; a program needn't handle non-finite values. No bound on the sum of `band_pattern` or of `slab_pattern` on one device may be relied on, other than what follows from the above.
Results may differ from a plain program's by a relative error of at most 0.0003.
Values sent between devices are 32-bit elements; how exact they have to be, the bound alone decides.
A program may use at most 64 MiB of HBM per device.

v0:
```python
import jax
import jax.numpy as jnp
from jax import lax
from jax.sharding import PartitionSpec as P

STEPS = 3


def passed_along(block, axis, distance):
    devices = range(lax.axis_size(axis))
    route = [((i - distance) % len(devices), i) for i in devices]
    return lax.ppermute(block, axis, route)


def spread(value, axis, source):
    kept = jnp.where(lax.axis_index(axis) == source, value, 0).astype(value.dtype)
    return lax.psum(kept, axis)


def masked_blocks(values, pattern, block):
    rows = pattern.shape[0]
    cols = pattern.shape[1]
    shaped = values.reshape(rows, block, cols, block)
    weights = pattern.astype(jnp.float32)[:, None, :, None]
    return (shaped * weights).reshape(rows * block, cols * block)


def per_device(band, band_pattern, slab, slab_pattern):
    block = band.shape[0] // band_pattern.shape[0]
    group_width = slab.shape[0]
    groups = lax.axis_size("col")
    per_holder = band.shape[1] // group_width
    column_index = lax.axis_index("col")
    masked_band = masked_blocks(band, band_pattern, block)
    masked_slab = masked_blocks(slab, slab_pattern, block)
    total = jnp.zeros((band.shape[0], slab.shape[1]), jnp.float32)
    right_pieces = [masked_slab]
    current = masked_slab
    for step in range(1, STEPS):
        current = passed_along(current, "col", -1)
        right_pieces.append(current)
    for step in range(STEPS):
        inner = (column_index + step) % groups
        holder = inner // per_holder
        chosen = lax.dynamic_slice_in_dim(
            masked_band, inner % per_holder * group_width, group_width, 1
        )
        left = spread(chosen, "row", holder)
        total = total + jnp.dot(
            left,
            right_pieces[step],
            preferred_element_type=jnp.float32,
            precision=lax.Precision.HIGHEST,
        )
    return total


def solution(mesh):
    placed = (P("col", "row"), P("col", "row"), P("col", "row"), P("col", "row"))
    return jax.shard_map(
        per_device, mesh=mesh, in_specs=placed, out_specs=P("col", "row"), check_vma=False
    )
```

profile of v0, /device:TPU:6, one launch (start us, length us, event | category | flops | bytes accessed | tf_op | source)
XLA Modules:
  0.0 186.9 jit_solution(4127702758515079536)
XLA Ops:
  6.5 0.0 all-reduce.3.cloned.1.call-start
  6.5 0.7 convert_element_type.10
  7.2 0.0 copy-start
  7.2 0.3 mul.31
  7.5 1.4 copy-done
  8.9 1.3 bitcast_multiply_fusion
  10.1 2.0 %dynamic-slice_select_fusion = (f32[384,768]{1,0:T(8,128)}, f32[384,768]{1,0:T(8,128)}, f32[384,768]{1,0:T(8,128)}) fusion(f32[384,1536]{1,0:T(8,128)S(1)} %bitcast_multiply_fusion, s32[]{:T(128)S(6)} %select_n.82, pred[]{:T(512)S(6)} %eq.18, s32[]{:T(128)S(6)} %select_n.76, pred[]{:T(512)S(6)} %eq.17, s32[]{:T(128)S(6)} %select_n.70, pred[]{:T(512)S(6)} %eq.16), kind=kLoop, calls=%fused_computation.4 | loop fusion | flops 884736 | bytes 7077903 | tf_op jit(solution)/shard_map/jit(_where)/select_n | solution.py:16
  12.1 0.0 copy-start.4
  12.1 0.0 all-reduce.3.cloned.1.call-update
  12.1 0.7 copy-done.4
  12.8 0.0 copy-start.1
  12.8 0.1 copy.6
  12.9 0.3 mul.35
  13.2 1.0 copy-done.1
  14.2 0.3 bitcast_multiply_fusion.1
  14.5 4.6 %collective-permute-start = (f32[768,512]{1,0:T(8,128)S(1)}, f32[768,512]{1,0:T(8,128)S(1)}, u32[]{:S(2)}, u32[]{:S(2)}) collective-permute-start(f32[768,512]{1,0:T(8,128)S(1)} %bitcast_multiply_fusion.1), channel_id=1, source_target_pairs={{1,0},{2,1},{3,2},{4,3},{5,4},{6,5},{7,6},{8,7},{9,8},{10,9},{11,1... | collective-permute-start | bytes 4718600 | tf_op jit(solution)/shard_map/ppermute | solution.py:12
  19.2 17.9 %collective-permute-done = f32[768,512]{1,0:T(8,128)S(1)} collective-permute-done((f32[768,512]{1,0:T(8,128)S(1)}, f32[768,512]{1,0:T(8,128)S(1)}, u32[]{:S(2)}, u32[]{:S(2)}) %collective-permute-start) | collective-permute-done | bytes 1572896 | tf_op jit(solution)/shard_map/ppermute | solution.py:12
  37.1 6.0 %collective-permute-start.1 = (f32[768,512]{1,0:T(8,128)S(1)}, f32[768,512]{1,0:T(8,128)}, u32[]{:S(2)}, u32[]{:S(2)}) collective-permute-start(f32[768,512]{1,0:T(8,128)S(1)} %collective-permute-done), channel_id=1, source_target_pairs={{1,0},{2,1},{3,2},{4,3},{5,4},{6,5},{7,6},{8,7},{9,8},{10,9},{11,1... | collective-permute-start | bytes 4718600 | tf_op jit(solution)/shard_map/ppermute | solution.py:12
  43.1 127.1 %all-reduce.3.cloned.1.call-done = (f32[384,768]{1,0:T(8,128)}, f32[384,768]{1,0:T(8,128)}, f32[384,768]{1,0:T(8,128)}) async-done(((f32[384,768]{1,0:T(8,128)}, f32[384,768]{1,0:T(8,128)}, f32[384,768]{1,0:T(8,128)}), (f32[384,768]{1,0:T(8,128)}, f32[384,768]{1,0:T(8,128)}, f32[384,768]{1,0:T(8,128)})) %all-reduce.3.cloned.1.call-update) | async-done | bytes 3538960 | tf_op jit(solution)/shard_map/psum | solution.py:17
  170.1 0.0 copy-start.3
  170.1 3.4 %fusion = f32[384,512]{1,0:T(8,128)S(1)} fusion(f32[384,768]{1,0:T(8,128)} %get-tuple-element.5, f32[768,512]{1,0:T(8,128)S(1)} %bitcast_multiply_fusion.1), kind=kOutput, calls=%fused_computation.7 | convolution fusion | flops 1811939328 | bytes 3538944 | tf_op jit(solution)/shard_map/dot_general | solution.py:49
  173.6 0.0 copy-done.3
  173.6 0.0 copy-start.2
  173.6 2.1 %convolution_add_fusion.1 = f32[384,512]{1,0:T(8,128)S(1)} fusion(f32[384,512]{1,0:T(8,128)S(1)} %fusion, f32[384,768]{1,0:T(8,128)S(1)} %copy-done.3, f32[768,512]{1,0:T(8,128)S(1)} %collective-permute-done), kind=kOutput, calls=%fused_computation.3 | convolution fusion | flops 1812135936 | bytes 4325376 | tf_op jit(solution)/shard_map/dot_general | solution.py:49
  175.7 0.0 collective-permute-done.1
  175.7 0.0 copy-done.2
  175.7 4.4 %convolution_add_fusion = f32[384,512]{1,0:T(8,128)} fusion(f32[384,512]{1,0:T(8,128)S(1)} %convolution_add_fusion.1, f32[384,768]{1,0:T(8,128)S(1)} %copy-done.2, f32[768,512]{1,0:T(8,128)} %collective-permute-done.1), kind=kOutput, calls=%fused_computation.2 | convolution fusion | flops 1812135936 | bytes 4325376 | tf_op jit(solution)/shard_map/dot_general | solution.py:49
  (1 shorter events, 0.0 us)
Async XLA Ops:
  6.5 163.6 %all-reduce.3.cloned.1.call-start = ((), (), s32[]{:S(2)}) async-start(), calls=%async_computation | async-start | bytes 7077888 | tf_op jit(solution)/shard_map/psum | solution.py:17
  7.2 1.7 copy-start
  12.1 0.7 copy-start.4
  12.8 1.4 copy-start.1
  14.5 22.5 %collective-permute-start = (f32[768,512]{1,0:T(8,128)S(1)}, f32[768,512]{1,0:T(8,128)S(1)}, u32[]{:S(2)}, u32[]{:S(2)}) collective-permute-start(f32[768,512]{1,0:T(8,128)S(1)} %bitcast_multiply_fusion.1), channel_id=1, source_target_pairs={{1,0},{2,1},{3,2},{4,3},{5,4},{6,5},{7,6},{8,7},{9,8},{10,9},{11,1... | collective-permute-start | bytes 4718600 | tf_op jit(solution)/shard_map/ppermute | solution.py:12
  37.1 138.6 %collective-permute-start.1 = (f32[768,512]{1,0:T(8,128)S(1)}, f32[768,512]{1,0:T(8,128)}, u32[]{:S(2)}, u32[]{:S(2)}) collective-permute-start(f32[768,512]{1,0:T(8,128)S(1)} %collective-permute-done), channel_id=1, source_target_pairs={{1,0},{2,1},{3,2},{4,3},{5,4},{6,5},{7,6},{8,7},{9,8},{10,9},{11,1... | collective-permute-start | bytes 4718600 | tf_op jit(solution)/shard_map/ppermute | solution.py:12
  170.1 3.5 %copy-start.3 = (f32[384,768]{1,0:T(8,128)S(1)}, f32[384,768]{1,0:T(8,128)}, u32[]{:S(2)}) copy-start(f32[384,768]{1,0:T(8,128)} %get-tuple-element.6) | copy-start | bytes 3538948
  173.6 2.1 %copy-start.2 = (f32[384,768]{1,0:T(8,128)S(1)}, f32[384,768]{1,0:T(8,128)}, u32[]{:S(2)}) copy-start(f32[384,768]{1,0:T(8,128)} %get-tuple-element.7) | copy-start | bytes 3538948
Sparse Core Ops, SparseCore 0:
  12.2 157.8 all-reduce.2
where the time goes:
time: 187 us
  waiting for transfers between devices  145 us (78%)
  between operations  13.5 us (7%)
  starting transfers between devices  10.6 us (6%)
  matrix products  9.93 us (5%)
  other arithmetic  4.24 us (2%)
  local copies, waits for them, and re-layouts  3.72 us (2%)
    psum x1, waiting for transfers between devices, spread(): return lax.psum(kept, axis)  127 us
    ppermute x2, waiting for transfers between devices, passed_along(): return lax.ppermute(block, axis, route)  17.9 us
    ppermute x2, starting transfers between devices, passed_along(): return lax.ppermute(block, axis, route)  10.6 us
    dot_general x3, matrix products, per_device(): jnp.dot(left, right_pieces[step], preferred_element_type=jnp.float32, pre...  9.93 us
  transfers between devices with their start and end apart: 3, of which 2 were waited for; matrix products, arithmetic and copies ran while one was open for 3% of the time, Pallas kernels for 0%

commit v1 on v0

v1 whole, which is shorter than its diff:
```python
import functools

import jax
import jax.numpy as jnp
from jax import lax
from jax.experimental import pallas as pl
from jax.experimental.pallas import tpu as pltpu
from jax.sharding import PartitionSpec as P

STEPS = 3
BLOCK = 128
PARTS = 4
ROWS = 8
OWN = 18
LAG = 3
LAGX = 1
FEEDS = 8
RELAY_AT = 20
RELAY_EVERY = 5
PASS_FROM = 22
PASS_EVERY = 2
PASS_LATE = 41
VMEM_MIB = 53
MESH = pl.DeviceIdType.MESH


def kernel(
    rows_n,
    cols_n,
    band_ref,
    band_pattern_ref,
    slab_ref,
    slab_pattern_ref,
    out_ref,
    left,
    carry,
    right,
    through,
    right_hi,
    right_lo,
    band_keep,
    slab_keep,
    load_sem,
    stream_recv,
    up_send,
    down_send,
    side_send,
    spread_send,
    side_recv,
    slab_send,
    slab_recv,
    through_send,
    through_recv,
    pass_send,
    pass_recv,
):
    row = lax.axis_index("row")
    col = lax.axis_index("col")
    height, depth = left.shape[1], left.shape[2]
    width = right.shape[2]
    per_holder = band_ref.shape[1] // depth
    across = cols_n // PARTS
    chunks = [OWN] + [carry.shape[2] // ROWS] * (PARTS - 1)
    begins = [0] + [OWN * ROWS + k * carry.shape[2] for k in range(PARTS - 1)]
    slots = max(chunks)
    core = lax.rem(col, 2)
    place = lax.rem(lax.div(col, 2), PARTS)
    sibling = col + 1 - 2 * core

    def column(offset):
        return lax.rem(col + (offset + cols_n), cols_n)

    up = lax.rem(row + 1, rows_n)
    down = lax.rem(row + rows_n - 1, rows_n)

    barrier = pltpu.get_barrier_semaphore()

    def greet(device):
        pl.semaphore_signal(barrier, inc=1, device_id=device, device_id_type=MESH)

    greet((up, col))
    greet((down, col))
    greet((row, sibling))
    greet((row, column(-2)))
    greet((row, column(2)))
    for k in range(1, PARTS):
        greet((row, column(across * k)))
    for where, offsets in ((0, (-6, -4, 6)), (1, (4, 6)), (2, (4,)), (3, (-6, -4))):

        @pl.when(place == where)
        def _():
            for offset in offsets:
                greet((row, column(offset)))

    greetings = 8 + jnp.where(place == 0, 3, jnp.where(place == 2, 1, 2))

    inner, away = [], {}
    reach = [rows_n // 2, rows_n // 2 - 1 + core, rows_n // 2 - 1]
    for s in range(STEPS):
        for i in range(PARTS):
            group = lax.rem(column(-across * i) + s, cols_n)
            away[i, s] = lax.rem(row - lax.div(group, per_holder) + rows_n, rows_n)
            if i == 0:
                inner.append(lax.rem(group, per_holder))

    def piece_load(s):
        return pltpu.make_async_copy(
            band_ref.at[:, pl.ds(pl.multiple_of(inner[s] * depth, depth), depth)],
            left.at[s],
            load_sem.at[s],
        )

    def other_loads():
        return (
            pltpu.make_async_copy(slab_ref, right.at[0], load_sem.at[STEPS]),
            pltpu.make_async_copy(band_pattern_ref, band_keep, load_sem.at[STEPS + 1]),
            pltpu.make_async_copy(slab_pattern_ref, slab_keep, load_sem.at[STEPS + 2]),
        )

    for s in range(STEPS):

        @pl.when(away[0, s] == 0)
        def _():
            piece_load(s).start()

    for copy in other_loads():
        copy.start()
    for copy in other_loads()[1:]:
        copy.wait()

    for s in range(STEPS):

        @pl.when(away[0, s] == 0)
        def _():
            piece_load(s).wait()
            for p in range(height // BLOCK):
                for q in range(depth // BLOCK):
                    keep = band_keep[p, inner[s] * (depth // BLOCK) + q]
                    at = (s, pl.ds(p * BLOCK, BLOCK), pl.ds(q * BLOCK, BLOCK))
                    left[at] = left[at] * keep.astype(jnp.float32)

    pl.semaphore_wait(barrier, greetings)

    def held(i, s, j, count=1):
        if i == 0:
            return left.at[s, pl.ds(pl.multiple_of(j * ROWS, ROWS), count * ROWS)]
        return carry.at[
            i - 1, s, pl.ds(pl.multiple_of(j * ROWS, ROWS), count * ROWS)
        ]

    def settled(i, s, j, count=1):
        at = pl.ds(pl.multiple_of(begins[i] + j * ROWS, ROWS), count * ROWS)
        return left.at[s, at]

    def remote(source, target, send, recv, device):
        return pltpu.make_async_remote_copy(
            src_ref=source,
            dst_ref=target,
            send_sem=send,
            recv_sem=recv,
            device_id=device,
            device_id_type=MESH,
        )

    def lift(i, s, j, count=1):
        block = held(i, s, j, count)
        return remote(
            block, block, up_send.at[i, s], stream_recv.at[i, s, j], (up, col)
        )

    def lower(i, s, j, count=1):
        block = held(i, s, j, count)
        return remote(
            block, block, down_send.at[i, s], stream_recv.at[i, s, j], (down, col)
        )

    def deliver(i, s, j, count=1):
        return remote(
            held(i, s, j, count),
            settled(i, s, j, count),
            side_send.at[i - 1, s],
            side_recv.at[i - 1, s],
            (row, column(-across * i)),
        )

    def spread(i, s, j, count=1):
        return remote(
            settled(i, s, j, count),
            held(i, s, j, count),
            spread_send.at[i - 1, s],
            stream_recv.at[i, s, j],
            (row, column(across * i)),
        )

    for s in range(STEPS):

        @pl.when(away[0, s] == 0)
        def _():
            for j in range(slots):
                for i in range(1, PARTS):
                    if j < chunks[i]:
                        spread(i, s, j).start()

    feed = right.shape[1] // FEEDS
    per_way = FEEDS // PARTS

    def slab_rows(m):
        return pl.ds(m * feed, feed)

    def slab_direct(m):
        return remote(
            right.at[0, slab_rows(m)],
            right.at[2, slab_rows(m)],
            slab_send.at[m],
            slab_recv.at[m],
            (row, column(-2)),
        )

    def slab_out(m):
        way = m // per_way
        return remote(
            right.at[0, slab_rows(m)],
            through.at[m % per_way],
            slab_send.at[m],
            through_recv.at[m % per_way],
            (row, column(2 * way - across)),
        )

    def slab_on(way, n):
        m = way * per_way + n
        return remote(
            through.at[n],
            right.at[2, slab_rows(m)],
            through_send.at[n],
            slab_recv.at[m],
            (row, column(across - 2 - 2 * way)),
        )

    def slab_pass(m, source):
        return remote(
            right.at[source, slab_rows(m)],
            right.at[1, slab_rows(m)],
            pass_send.at[m],
            pass_recv.at[m],
            (row, sibling),
        )

    other_loads()[0].wait()

    def feed_slab(m):
        for p in range(m * feed // BLOCK, -(-(m + 1) * feed // BLOCK)):
            first, last = max(m * feed, p * BLOCK), min((m + 1) * feed, (p + 1) * BLOCK)
            for n in range(width // BLOCK):
                keep = slab_keep[n, p]
                at = (0, pl.ds(first, last - first), pl.ds(n * BLOCK, BLOCK))
                right[at] = right[at] * keep.astype(jnp.float32)
        if m >= FEEDS - per_way:
            slab_direct(m).start()
        else:

            @pl.when(place == 0)
            def _():
                slab_out(m).start()

            @pl.when(place > 0)
            def _():
                slab_direct(m).start()

        @pl.when(core == 1)
        def _():
            slab_pass(m, 0).start()

    def split(s):
        value = right[s]
        high = value.astype(jnp.bfloat16)
        right_hi[s] = high
        right_lo[s] = (value - high.astype(jnp.float32)).astype(jnp.bfloat16)

    def relay_slab(way):
        for n in range(per_way):
            slab_out(way * per_way + n).wait_recv()
            slab_on(way, n).start()

    def pass_slab(m):
        slab_direct(m).wait_recv()

        @pl.when(core == 0)
        def _():
            slab_pass(m, 2).start()

    half = rows_n // 4
    late = PASS_LATE

    def step(t, carried):
        for s in range(STEPS):
            for i in range(PARTS):
                steps = away[i, s]
                rising = steps <= reach[s]
                distance = jnp.where(rising, steps, rows_n - steps)
                j = t - jnp.where(
                    distance < half, distance * LAG, slots + (distance - half) * LAG
                )
                if i > 0:
                    j = j - LAGX

                @pl.when((j >= 0) & (j < chunks[i]))
                def _():
                    def arrived():
                        lift(i, s, j).wait_recv()

                    if i == 0:
                        pl.when(steps > 0)(arrived)
                    else:
                        arrived()

                    @pl.when(steps < reach[s])
                    def _():
                        lift(i, s, j).start()

                    @pl.when((steps == 0) | (steps > reach[s] + 1))
                    def _():
                        lower(i, s, j).start()

                    if i > 0:

                        @pl.when(steps > 0)
                        def _():
                            deliver(i, s, j).start()

        for m in range(FEEDS):

            @pl.when(t == m)
            def _():
                feed_slab(m)

            @pl.when(t == jnp.where(place == PARTS - 1, late + m, PASS_FROM + PASS_EVERY * m))
            def _():
                pass_slab(m)

        for way in range(PARTS - 1):

            @pl.when((t == RELAY_AT + RELAY_EVERY * way) & (place == way))
            def _():
                relay_slab(way)

        @pl.when(t == FEEDS)
        def _():
            split(0)

        return carried

    total_steps = max(
        2 * slots + LAG * (half + 1) + LAGX,
        PASS_FROM + PASS_EVERY * (FEEDS - 1) + 1,
        PASS_LATE + FEEDS,
        RELAY_AT + RELAY_EVERY * (PARTS - 2) + 1,
    )
    lax.fori_loop(0, total_steps, step, 0)

    for m in range(FEEDS):
        slab_pass(m, 0).wait_recv()
    split(1)
    split(2)

    for i in range(PARTS):
        for s in range(STEPS):
            if i > 0:

                @pl.when(away[0, s] > 0)
                def _():
                    deliver(i, s, 0, chunks[i]).wait_recv()

        at = pl.ds(begins[i], chunks[i] * ROWS)
        total = jnp.zeros((chunks[i] * ROWS, width), jnp.float32)
        for s in range(STEPS):
            value = left[s, at]
            high = value.astype(jnp.bfloat16)
            low = (value - high.astype(jnp.float32)).astype(jnp.bfloat16)
            for a, b in ((high, right_hi), (high, right_lo), (low, right_hi)):
                total = total + jnp.dot(a, b[s], preferred_element_type=jnp.float32)
        out_ref[at] = total

    for m in range(FEEDS):
        slab_direct(m).wait_send()
        slab_pass(m, 0).wait_send()
    for way in range(PARTS - 1):

        @pl.when(place == way)
        def _():
            for n in range(per_way):
                slab_on(way, n).wait_send()

    for s in range(STEPS):
        for i in range(PARTS):
            steps = away[i, s]

            @pl.when(steps < reach[s])
            def _():
                lift(i, s, 0, chunks[i]).wait_send()

            @pl.when((steps == 0) | (steps > reach[s] + 1))
            def _():
                lower(i, s, 0, chunks[i]).wait_send()

            if i > 0:

                @pl.when(steps > 0)
                def _():
                    deliver(i, s, 0, chunks[i]).wait_send()

                @pl.when(away[0, s] == 0)
                def _():
                    spread(i, s, 0, chunks[i]).wait_send()


def per_device(band, band_pattern, slab, slab_pattern):
    rows_n, cols_n = lax.axis_size("row"), lax.axis_size("col")
    height = band.shape[0]
    depth, width = slab.shape
    part = (height - OWN * ROWS) // (PARTS - 1)
    slots = max(OWN, part // ROWS)
    anywhere = pl.BlockSpec(memory_space=pl.ANY)
    dma = pltpu.SemaphoreType.DMA
    return pl.pallas_call(
        functools.partial(kernel, rows_n, cols_n),
        out_shape=jax.ShapeDtypeStruct((height, width), jnp.float32),
        in_specs=[anywhere] * 4,
        out_specs=pl.BlockSpec(memory_space=pltpu.VMEM),
        scratch_shapes=[
            pltpu.VMEM((STEPS, height, depth), jnp.float32),
            pltpu.VMEM((PARTS - 1, STEPS, part, depth), jnp.float32),
            pltpu.VMEM((STEPS, depth, width), jnp.float32),
            pltpu.VMEM((FEEDS // PARTS, depth // FEEDS, width), jnp.float32),
            pltpu.VMEM((STEPS, depth, width), jnp.bfloat16),
            pltpu.VMEM((STEPS, depth, width), jnp.bfloat16),
            pltpu.SMEM(band_pattern.shape, jnp.int32),
            pltpu.SMEM(slab_pattern.shape[::-1], jnp.int32),
            dma((STEPS + 3,)),
            dma((PARTS, STEPS, slots)),
            dma((PARTS, STEPS)),
            dma((PARTS, STEPS)),
            dma((PARTS - 1, STEPS)),
            dma((PARTS - 1, STEPS)),
            dma((PARTS - 1, STEPS)),
            dma((FEEDS,)),
            dma((FEEDS,)),
            dma((FEEDS // PARTS,)),
            dma((FEEDS // PARTS,)),
            dma((FEEDS,)),
            dma((FEEDS,)),
        ],
        compiler_params=pltpu.CompilerParams(
            collective_id=0, has_side_effects=True, vmem_limit_bytes=VMEM_MIB * 1024 * 1024
        ),
        cost_estimate=pl.CostEstimate(
            flops=2 * STEPS * height * depth * width,
            bytes_accessed=4 * (band.size + slab.size + height * width),
            transcendentals=0,
        ),
    )(band, band_pattern, slab, slab_pattern.T)


def solution(mesh):
    placed = (P("col", "row"), P("col", "row"), P("col", "row"), P("col", "row"))
    return jax.shard_map(
        per_device, mesh=mesh, in_specs=placed, out_specs=P("col", "row"), check_vma=False
    )
```

time: 187 us -> 98.3 us (0.53)
  the two profiles are of different devices: /device:TPU:6 before, /device:TPU:386 now
where the time goes in v1:
time: 98.3 us; the launch traced here: 98.1 us
  Pallas kernels  95.8 us (97%)
  local copies, waits for them, and re-layouts  2.24 us (2%)
    pallas_call x1, Pallas kernels, per_device(): pl.pallas_call(functools.partial(kernel, rows_n, cols_n), out_shape=jax.S...  95.8 us
    unnamed x5, local copies, waits for them, and re-layouts  2.24 us

profile of v1, /device:TPU:386, one launch (start us, length us, event | category | flops | bytes accessed | tf_op | source)
XLA Modules:
  0.0 98.1 jit_solution(3748118549966017596)
XLA Ops:
  0.0 0.0 copy-start
  0.0 0.7 copy-done
  0.7 0.0 copy-start.1
  0.7 0.7 copy-done.1
  1.4 95.8 %shard_map.46 = f32[384,512]{1,0:T(8,128)S(1)} custom-call(f32[384,1536]{1,0:T(8,128)} %band_ref.1, s32[3,12]{1,0:T(4,128)S(1)} %copy-done, f32[768,512]{1,0:T(8,128)} %slab_ref.1, s32[4,6]{1,0:T(4,128)S(1)} %bitcast.1), custom_call_target="tpu_custom_call" | custom-call | flops 905969664 | bytes 4718592 | tf_op jit(solution)/shard_map/pallas_call | solution.py:424
  97.2 0.9 copy.6
Async XLA Ops:
  0.0 0.7 copy-start
  0.7 0.7 copy-start.1

commit v2 on v1

--- a/solution.py
+++ b/solution.py
@@ -11,15 +11,17 @@
 BLOCK = 128
 PARTS = 4
 ROWS = 8
-OWN = 18
+CHUNKS = (18, 12, 6, 12)
 LAG = 3
+FAR = 12
 LAGX = 1
+LATE = (3,)
 FEEDS = 8
-RELAY_AT = 20
-RELAY_EVERY = 5
-PASS_FROM = 22
+RELAY_AT = (12, 14, 18)
+FEED_AT = (0, 1, 2, 3, 4, 5, 12, 14)
+PASS_FROM = 18
 PASS_EVERY = 2
-PASS_LATE = 41
+PASS_LATE = 37
 VMEM_MIB = 53
 MESH = pl.DeviceIdType.MESH
 
@@ -60,8 +62,8 @@
     width = right.shape[2]
     per_holder = band_ref.shape[1] // depth
     across = cols_n // PARTS
-    chunks = [OWN] + [carry.shape[2] // ROWS] * (PARTS - 1)
-    begins = [0] + [OWN * ROWS + k * carry.shape[2] for k in range(PARTS - 1)]
+    chunks = CHUNKS
+    begins = [sum(chunks[:i]) * ROWS for i in range(PARTS)]
     slots = max(chunks)
     core = lax.rem(col, 2)
     place = lax.rem(lax.div(col, 2), PARTS)
@@ -85,14 +87,14 @@
     greet((row, column(2)))
     for k in range(1, PARTS):
         greet((row, column(across * k)))
-    for where, offsets in ((0, (-6, -4, 6)), (1, (4, 6)), (2, (4,)), (3, (-6, -4))):
+    for where, offsets in ((0, (4, 6)), (1, (-4,)), (2, (-4, -6)), (3, (-6, 4, 6))):
 
         @pl.when(place == where)
         def _():
             for offset in offsets:
                 greet((row, column(offset)))
 
-    greetings = 8 + jnp.where(place == 0, 3, jnp.where(place == 2, 1, 2))
+    greetings = 8 + jnp.where(place == 3, 3, jnp.where(place == 1, 1, 2))
 
     inner, away = [], {}
     reach = [rows_n // 2, rows_n // 2 - 1 + core, rows_n // 2 - 1]
@@ -128,17 +130,6 @@
     for copy in other_loads()[1:]:
         copy.wait()
 
-    for s in range(STEPS):
-
-        @pl.when(away[0, s] == 0)
-        def _():
-            piece_load(s).wait()
-            for p in range(height // BLOCK):
-                for q in range(depth // BLOCK):
-                    keep = band_keep[p, inner[s] * (depth // BLOCK) + q]
-                    at = (s, pl.ds(p * BLOCK, BLOCK), pl.ds(q * BLOCK, BLOCK))
-                    left[at] = left[at] * keep.astype(jnp.float32)
-
     pl.semaphore_wait(barrier, greetings)
 
     def held(i, s, j, count=1):
@@ -192,14 +183,13 @@
             (row, column(across * i)),
         )
 
-    for s in range(STEPS):
-
-        @pl.when(away[0, s] == 0)
-        def _():
-            for j in range(slots):
-                for i in range(1, PARTS):
-                    if j < chunks[i]:
-                        spread(i, s, j).start()
+    def mask_band(i, s, j):
+        rows = begins[i] + j * ROWS
+        p = lax.div(rows, BLOCK)
+        for q in range(depth // BLOCK):
+            keep = band_keep[p, inner[s] * (depth // BLOCK) + q]
+            at = (s, pl.ds(pl.multiple_of(rows, ROWS), ROWS), pl.ds(q * BLOCK, BLOCK))
+            left[at] = left[at] * keep.astype(jnp.float32)
 
     feed = right.shape[1] // FEEDS
     per_way = FEEDS // PARTS
@@ -223,7 +213,7 @@
             through.at[m % per_way],
             slab_send.at[m],
             through_recv.at[m % per_way],
-            (row, column(2 * way - across)),
+            (row, column(2 * way)),
         )
 
     def slab_on(way, n):
@@ -233,7 +223,7 @@
             right.at[2, slab_rows(m)],
             through_send.at[n],
             slab_recv.at[m],
-            (row, column(across - 2 - 2 * way)),
+            (row, column(-2 * way - 2)),
         )
 
     def slab_pass(m, source):
@@ -254,7 +244,7 @@
                 keep = slab_keep[n, p]
                 at = (0, pl.ds(first, last - first), pl.ds(n * BLOCK, BLOCK))
                 right[at] = right[at] * keep.astype(jnp.float32)
-        if m >= FEEDS - per_way:
+        if m < per_way:
             slab_direct(m).start()
         else:
 
@@ -289,19 +279,42 @@
             slab_pass(m, 2).start()
 
     half = rows_n // 4
+    first = {}
+    for i, s in away:
+        steps = away[i, s]
+        distance = jnp.where(steps <= reach[s], steps, rows_n - steps)
+        first[i, s] = jnp.where(
+            distance < half, distance * LAG, FAR + (distance - half) * LAG
+        ) + (LAGX if i > 0 else 0)
+
+    for s in range(STEPS):
+
+        @pl.when(away[0, s] == 0)
+        def _():
+            piece_load(s).wait()
+
     late = PASS_LATE
+    is_late = place == LATE[0]
+    for other in LATE[1:]:
+        is_late = is_late | (place == other)
 
     def step(t, carried):
+        for s in range(STEPS):
+
+            @pl.when((away[0, s] == 0) & (t < slots))
+            def _():
+                for i in range(PARTS):
+
+                    @pl.when(t < chunks[i])
+                    def _():
+                        mask_band(i, s, t)
+                        if i > 0:
+                            spread(i, s, t).start()
+
         for s in range(STEPS):
             for i in range(PARTS):
                 steps = away[i, s]
-                rising = steps <= reach[s]
-                distance = jnp.where(rising, steps, rows_n - steps)
-                j = t - jnp.where(
-                    distance < half, distance * LAG, slots + (distance - half) * LAG
-                )
-                if i > 0:
-                    j = j - LAGX
+                j = t - first[i, s]
 
                 @pl.when((j >= 0) & (j < chunks[i]))
                 def _():
@@ -327,33 +340,34 @@
                         def _():
                             deliver(i, s, j).start()
 
-        for m in range(FEEDS):
-
-            @pl.when(t == m)
+        for n in range(FEEDS):
+            m = (n + per_way) % FEEDS
+
+            @pl.when(t == FEED_AT[n])
             def _():
                 feed_slab(m)
 
-            @pl.when(t == jnp.where(place == PARTS - 1, late + m, PASS_FROM + PASS_EVERY * m))
+            @pl.when(t == jnp.where(is_late, late + n, PASS_FROM + PASS_EVERY * n))
             def _():
                 pass_slab(m)
 
-        for way in range(PARTS - 1):
-
-            @pl.when((t == RELAY_AT + RELAY_EVERY * way) & (place == way))
+        for way in range(1, PARTS):
+
+            @pl.when((t == RELAY_AT[way - 1]) & (place == way))
             def _():
                 relay_slab(way)
 
-        @pl.when(t == FEEDS)
+        @pl.when(t == FEED_AT[-1] + 1)
         def _():
             split(0)
 
         return carried
 
     total_steps = max(
-        2 * slots + LAG * (half + 1) + LAGX,
+        FAR + slots + LAG * (half + 1) + LAGX,
         PASS_FROM + PASS_EVERY * (FEEDS - 1) + 1,
         PASS_LATE + FEEDS,
-        RELAY_AT + RELAY_EVERY * (PARTS - 2) + 1,
+        max(RELAY_AT) + 1,
     )
     lax.fori_loop(0, total_steps, step, 0)
 
@@ -383,7 +397,7 @@
     for m in range(FEEDS):
         slab_direct(m).wait_send()
         slab_pass(m, 0).wait_send()
-    for way in range(PARTS - 1):
+    for way in range(1, PARTS):
 
         @pl.when(place == way)
         def _():
@@ -417,8 +431,8 @@
     rows_n, cols_n = lax.axis_size("row"), lax.axis_size("col")
     height = band.shape[0]
     depth, width = slab.shape
-    part = (height - OWN * ROWS) // (PARTS - 1)
-    slots = max(OWN, part // ROWS)
+    part = max(CHUNKS[1:]) * ROWS
+    slots = max(CHUNKS)
     anywhere = pl.BlockSpec(memory_space=pl.ANY)
     dma = pltpu.SemaphoreType.DMA
     return pl.pallas_call(

time: 98.3 us -> 87.2 us (0.89)
  the two profiles are of different devices: /device:TPU:386 before, /device:TPU:26 now
where the time goes in v2:
time: 87.2 us; the launch traced here: 87.1 us
  Pallas kernels  84.8 us (97%)
  local copies, waits for them, and re-layouts  2.24 us (3%)
    pallas_call x1, Pallas kernels, per_device(): pl.pallas_call(functools.partial(kernel, rows_n, cols_n), out_shape=jax.S...  84.8 us
    unnamed x5, local copies, waits for them, and re-layouts  2.24 us

profile of v2, /device:TPU:26, one launch (start us, length us, event | category | flops | bytes accessed | tf_op | source)
XLA Modules:
  0.0 87.1 jit_solution(17842209421441120126)
XLA Ops:
  0.0 0.0 copy-start
  0.0 0.7 copy-done
  0.7 0.0 copy-start.1
  0.7 0.7 copy-done.1
  1.4 84.8 %shard_map.46 = f32[384,512]{1,0:T(8,128)S(1)} custom-call(f32[384,1536]{1,0:T(8,128)} %band_ref.1, s32[3,12]{1,0:T(4,128)S(1)} %copy-done, f32[768,512]{1,0:T(8,128)} %slab_ref.1, s32[4,6]{1,0:T(4,128)S(1)} %bitcast.1), custom_call_target="tpu_custom_call" | custom-call | flops 905969664 | bytes 4718592 | tf_op jit(solution)/shard_map/pallas_call | solution.py:438
  86.2 0.9 %copy.6 = f32[384,512]{1,0:T(8,128)} copy(f32[384,512]{1,0:T(8,128)S(1)} %shard_map.46) | data formatting | bytes 1572864
Async XLA Ops:
  0.0 0.7 copy-start
  0.7 0.7 copy-start.1

commit v3 on v2

--- a/solution.py
+++ b/solution.py
@@ -12,16 +12,17 @@
 PARTS = 4
 ROWS = 8
 CHUNKS = (18, 12, 6, 12)
+SOON = (8, 6, 4, 6)
+SOON_AT = 39
 LAG = 3
 FAR = 12
 LAGX = 1
-LATE = (3,)
 FEEDS = 8
 RELAY_AT = (12, 14, 18)
-FEED_AT = (0, 1, 2, 3, 4, 5, 12, 14)
+FEED_AT = (0, 1, 2, 3, 4, 5, 16, 19)
 PASS_FROM = 18
 PASS_EVERY = 2
-PASS_LATE = 37
+PASS_LATE = 31
 VMEM_MIB = 53
 MESH = pl.DeviceIdType.MESH
 
@@ -165,12 +166,12 @@
             block, block, down_send.at[i, s], stream_recv.at[i, s, j], (down, col)
         )
 
-    def deliver(i, s, j, count=1):
+    def deliver(i, s, j, count=1, tail=0):
         return remote(
             held(i, s, j, count),
             settled(i, s, j, count),
             side_send.at[i - 1, s],
-            side_recv.at[i - 1, s],
+            side_recv.at[i - 1, s, tail],
             (row, column(-across * i)),
         )
 
@@ -195,7 +196,8 @@
     per_way = FEEDS // PARTS
 
     def slab_rows(m):
-        return pl.ds(m * feed, feed)
+        start = m * feed
+        return pl.ds(start if isinstance(m, int) else pl.multiple_of(start, 8), feed)
 
     def slab_direct(m):
         return remote(
@@ -266,6 +268,32 @@
         right_hi[s] = high
         right_lo[s] = (value - high.astype(jnp.float32)).astype(jnp.bfloat16)
 
+    def multiply(s, tail):
+        places = []
+        for i in range(PARTS):
+            j = SOON[i] if tail else 0
+            count = chunks[i] - SOON[i] if tail else SOON[i]
+            places.append(pl.ds(begins[i] + j * ROWS, count * ROWS))
+            if i > 0:
+
+                @pl.when(away[0, s] > 0)
+                def _():
+                    deliver(i, s, j, count, tail).wait_recv()
+
+        value = jnp.concatenate([left[s, at] for at in places], axis=0)
+        high = value.astype(jnp.bfloat16)
+        low = (value - high.astype(jnp.float32)).astype(jnp.bfloat16)
+        if s == 0:
+            total = jnp.zeros((value.shape[0], width), jnp.float32)
+        else:
+            total = jnp.concatenate([out_ref[at] for at in places], axis=0)
+        for a, b in ((high, right_hi), (high, right_lo), (low, right_hi)):
+            total = total + jnp.dot(a, b[s], preferred_element_type=jnp.float32)
+        begin = 0
+        for at in places:
+            out_ref[at] = total[begin : begin + at.size]
+            begin += at.size
+
     def relay_slab(way):
         for n in range(per_way):
             slab_out(way * per_way + n).wait_recv()
@@ -293,23 +321,27 @@
         def _():
             piece_load(s).wait()
 
-    late = PASS_LATE
-    is_late = place == LATE[0]
-    for other in LATE[1:]:
-        is_late = is_late | (place == other)
+    pass_from = jnp.where(place == PARTS - 1, PASS_LATE, PASS_FROM)
+    pass_every = jnp.where(place == PARTS - 1, 1, PASS_EVERY)
+    relay_at = jnp.int32(-1)
+    for way in range(1, PARTS):
+        relay_at = jnp.where(place == way, RELAY_AT[way - 1], relay_at)
+    is_holder = (away[0, 0] == 0) | (away[0, 1] == 0) | (away[0, 2] == 0)
 
     def step(t, carried):
-        for s in range(STEPS):
-
-            @pl.when((away[0, s] == 0) & (t < slots))
-            def _():
-                for i in range(PARTS):
-
-                    @pl.when(t < chunks[i])
-                    def _():
-                        mask_band(i, s, t)
-                        if i > 0:
-                            spread(i, s, t).start()
+        @pl.when(is_holder & (t < slots))
+        def _():
+            for s in range(STEPS):
+
+                @pl.when(away[0, s] == 0)
+                def _():
+                    for i in range(PARTS):
+
+                        @pl.when(t < chunks[i])
+                        def _():
+                            mask_band(i, s, t)
+                            if i > 0:
+                                spread(i, s, t).start()
 
         for s in range(STEPS):
             for i in range(PARTS):
@@ -338,28 +370,46 @@
 
                         @pl.when(steps > 0)
                         def _():
-                            deliver(i, s, j).start()
-
-        for n in range(FEEDS):
-            m = (n + per_way) % FEEDS
-
-            @pl.when(t == FEED_AT[n])
+                            deliver(i, s, j, 1, jnp.where(j < SOON[i], 0, 1)).start()
+
+        @pl.when(t <= FEED_AT[-1] + 1)
+        def _():
+            for n in range(FEEDS):
+
+                @pl.when(t == FEED_AT[n])
+                def _():
+                    feed_slab((n + per_way) % FEEDS)
+
+            @pl.when(t == FEED_AT[-1] + 1)
             def _():
-                feed_slab(m)
-
-            @pl.when(t == jnp.where(is_late, late + n, PASS_FROM + PASS_EVERY * n))
-            def _():
-                pass_slab(m)
-
-        for way in range(1, PARTS):
-
-            @pl.when((t == RELAY_AT[way - 1]) & (place == way))
-            def _():
-                relay_slab(way)
-
-        @pl.when(t == FEED_AT[-1] + 1)
-        def _():
-            split(0)
+                split(0)
+
+        n = lax.div(t - pass_from, pass_every)
+
+        @pl.when((t >= pass_from) & (n < FEEDS) & (n * pass_every == t - pass_from))
+        def _():
+            pass_slab(lax.rem(n + per_way, FEEDS))
+
+        @pl.when((t >= min(RELAY_AT)) & (t == relay_at))
+        def _():
+            for way in range(1, PARTS):
+
+                @pl.when(place == way)
+                def _():
+                    relay_slab(way)
+
+        @pl.when(t >= SOON_AT)
+        def _():
+            for s in range(STEPS):
+
+                @pl.when(t == SOON_AT + s)
+                def _():
+                    if s == 1:
+                        for m in range(FEEDS):
+                            slab_pass(m, 0).wait_recv()
+                    if s > 0:
+                        split(s)
+                    multiply(s, 0)
 
         return carried
 
@@ -367,32 +417,13 @@
         FAR + slots + LAG * (half + 1) + LAGX,
         PASS_FROM + PASS_EVERY * (FEEDS - 1) + 1,
         PASS_LATE + FEEDS,
+        SOON_AT + STEPS,
         max(RELAY_AT) + 1,
     )
     lax.fori_loop(0, total_steps, step, 0)
 
-    for m in range(FEEDS):
-        slab_pass(m, 0).wait_recv()
-    split(1)
-    split(2)
-
-    for i in range(PARTS):
-        for s in range(STEPS):
-            if i > 0:
-
-                @pl.when(away[0, s] > 0)
-                def _():
-                    deliver(i, s, 0, chunks[i]).wait_recv()
-
-        at = pl.ds(begins[i], chunks[i] * ROWS)
-        total = jnp.zeros((chunks[i] * ROWS, width), jnp.float32)
-        for s in range(STEPS):
-            value = left[s, at]
-            high = value.astype(jnp.bfloat16)
-            low = (value - high.astype(jnp.float32)).astype(jnp.bfloat16)
-            for a, b in ((high, right_hi), (high, right_lo), (low, right_hi)):
-                total = total + jnp.dot(a, b[s], preferred_element_type=jnp.float32)
-        out_ref[at] = total
+    for s in range(STEPS):
+        multiply(s, 1)
 
     for m in range(FEEDS):
         slab_direct(m).wait_send()
@@ -455,7 +486,7 @@
             dma((PARTS, STEPS)),
             dma((PARTS - 1, STEPS)),
             dma((PARTS - 1, STEPS)),
-            dma((PARTS - 1, STEPS)),
+            dma((PARTS - 1, STEPS, 2)),
             dma((FEEDS,)),
             dma((FEEDS,)),
             dma((FEEDS // PARTS,)),

time: 87.2 us -> 84.5 us (0.969)
  Pallas kernels: 84.8 us -> 81.8 us
    pallas_call x1, Pallas kernels: 84.8 us -> 81.8 us  [per_device(): pl.pallas_call(functools.partial(kernel, rows_n, cols_n), out_shape=jax.S...]
where the time goes in v3:
time: 84.5 us; the launch traced here: 84.1 us
  Pallas kernels  81.8 us (97%)
  local copies, waits for them, and re-layouts  2.24 us (3%)
    pallas_call x1, Pallas kernels, per_device(): pl.pallas_call(functools.partial(kernel, rows_n, cols_n), out_shape=jax.S...  81.8 us
    unnamed x5, local copies, waits for them, and re-layouts  2.24 us

profile of v3, /device:TPU:26, one launch (start us, length us, event | category | flops | bytes accessed | tf_op | source)
XLA Modules:
  0.0 84.1 jit_solution(13334267400540378512)
XLA Ops:
  0.0 0.0 copy-start
  0.0 0.7 copy-done
  0.7 0.0 copy-start.1
  0.7 0.7 copy-done.1
  1.4 81.8 %shard_map.46 = f32[384,512]{1,0:T(8,128)S(1)} custom-call(f32[384,1536]{1,0:T(8,128)} %band_ref.1, s32[3,12]{1,0:T(4,128)S(1)} %copy-done, f32[768,512]{1,0:T(8,128)} %slab_ref.1, s32[4,6]{1,0:T(4,128)S(1)} %bitcast.1), custom_call_target="tpu_custom_call" | custom-call | flops 905969664 | bytes 4718592 | tf_op jit(solution)/shard_map/pallas_call | solution.py:469
  83.2 0.9 %copy.6 = f32[384,512]{1,0:T(8,128)} copy(f32[384,512]{1,0:T(8,128)S(1)} %shard_map.46) | data formatting | bytes 1572864
Async XLA Ops:
  0.0 0.7 copy-start
  0.7 0.7 copy-start.1

commit v4 on v3

--- a/solution.py
+++ b/solution.py
@@ -307,13 +307,16 @@
             slab_pass(m, 2).start()
 
     half = rows_n // 4
-    first = {}
+    first, rises, falls, foreign = {}, {}, {}, {}
     for i, s in away:
         steps = away[i, s]
         distance = jnp.where(steps <= reach[s], steps, rows_n - steps)
         first[i, s] = jnp.where(
             distance < half, distance * LAG, FAR + (distance - half) * LAG
         ) + (LAGX if i > 0 else 0)
+        rises[i, s] = steps < reach[s]
+        falls[i, s] = (steps == 0) | (steps > reach[s] + 1)
+        foreign[i, s] = steps > 0
 
     for s in range(STEPS):
 
@@ -345,7 +348,6 @@
 
         for s in range(STEPS):
             for i in range(PARTS):
-                steps = away[i, s]
                 j = t - first[i, s]
 
                 @pl.when((j >= 0) & (j < chunks[i]))
@@ -354,21 +356,21 @@
                         lift(i, s, j).wait_recv()
 
                     if i == 0:
-                        pl.when(steps > 0)(arrived)
+                        pl.when(foreign[i, s])(arrived)
                     else:
                         arrived()
 
-                    @pl.when(steps < reach[s])
+                    @pl.when(rises[i, s])
                     def _():
                         lift(i, s, j).start()
 
-                    @pl.when((steps == 0) | (steps > reach[s] + 1))
+                    @pl.when(falls[i, s])
                     def _():
                         lower(i, s, j).start()
 
                     if i > 0:
 
-                        @pl.when(steps > 0)
+                        @pl.when(foreign[i, s])
                         def _():
                             deliver(i, s, j, 1, jnp.where(j < SOON[i], 0, 1)).start()
 
@@ -414,7 +416,7 @@
         return carried
 
     total_steps = max(
-        FAR + slots + LAG * (half + 1) + LAGX,
+        FAR + LAG * half + max(chunks[0], max(chunks[1:]) + LAGX),
         PASS_FROM + PASS_EVERY * (FEEDS - 1) + 1,
         PASS_LATE + FEEDS,
         SOON_AT + STEPS,

time: 84.5 us -> 84.2 us (level)
  no operation moved by 1% of the time
where the time goes in v4:
time: 84.2 us; the launch traced here: 84.1 us
  Pallas kernels  81.8 us (97%)
  local copies, waits for them, and re-layouts  2.24 us (3%)
    pallas_call x1, Pallas kernels, per_device(): pl.pallas_call(functools.partial(kernel, rows_n, cols_n), out_shape=jax.S...  81.8 us
    unnamed x5, local copies, waits for them, and re-layouts  2.24 us

profile of v4, /device:TPU:26, one launch (start us, length us, event | category | flops | bytes accessed | tf_op | source)
XLA Modules:
  0.0 84.1 jit_solution(45036351345067246)
XLA Ops:
  0.0 0.0 copy-start
  0.0 0.7 copy-done
  0.7 0.0 copy-start.1
  0.7 0.7 copy-done.1
  1.4 81.8 %shard_map.46 = f32[384,512]{1,0:T(8,128)S(1)} custom-call(f32[384,1536]{1,0:T(8,128)} %band_ref.1, s32[3,12]{1,0:T(4,128)S(1)} %copy-done, f32[768,512]{1,0:T(8,128)} %slab_ref.1, s32[4,6]{1,0:T(4,128)S(1)} %bitcast.1), custom_call_target="tpu_custom_call" | custom-call | flops 905969664 | bytes 4718592 | tf_op jit(solution)/shard_map/pallas_call | solution.py:471
  83.2 0.9 %copy.6 = f32[384,512]{1,0:T(8,128)} copy(f32[384,512]{1,0:T(8,128)S(1)} %shard_map.46) | data formatting | bytes 1572864
Async XLA Ops:
  0.0 0.7 copy-start
  0.7 0.7 copy-start.1
